TPU v7x, 256 devices: a whole 4x4x8 slice. The times are simulated.
256 devices in a mesh: pair: 8 (over y_hi, x), row: 32 (over y_lo, z, core).
Axes of the slice: x: 4, y: 4 (y_hi: 2, y_lo: 2; y = y_hi * 2 + y_lo), z: 8, core: 2. Of those that a mesh axis runs over, the one named last changes fastest.
Arguments:
- snapshots: float32 [65536, 2048], P('row', 'pair'), may hold values from -13 to 13
Outputs:
- rotated: float32 [65536, 2048], P('row', 'pair')
All inputs are finite; a program needn't handle non-finite values.
Results may differ from a plain program's by a relative error of at most 0.0003.
Values sent between devices are 32-bit elements; how exact they have to be, the bound alone decides.
A program may use at most 64 MiB of HBM per device.

v0:
```python
import jax
import jax.numpy as jnp
from jax import lax
from jax.sharding import PartitionSpec as P

ROUNDS = 3
INNER = 2


highest = lax.Precision.HIGHEST


def from_behind(array, axis, by):
    size = lax.axis_size(axis)
    pairs = [(i, i + by) for i in range(size) if 0 <= i + by < size]
    return lax.ppermute(array, axis, pairs)


def eigen_rotation(gram_full):
    extent = gram_full.shape[0]
    rotation = jnp.eye(extent, dtype=gram_full.dtype)
    for repeat in range(INNER):
        images = jnp.dot(gram_full, rotation, precision=highest)
        crossed = jnp.einsum("ki,kj->ij", images, images, precision=highest)
        factor = jnp.linalg.cholesky(crossed)
        rotation = lax.linalg.triangular_solve(
            factor, images, left_side=False, lower=True, transpose_a=True
        )
    return rotation


def block_products(top_block, low_block):
    top_gram = jnp.einsum("mi,mj->ij", top_block, top_block, precision=highest)
    cross_gram = jnp.einsum("mi,mj->ij", top_block, low_block, precision=highest)
    low_gram = jnp.einsum("mi,mj->ij", low_block, low_block, precision=highest)
    return (top_gram, cross_gram, low_gram)


def assemble(top_gram, cross_gram, low_gram):
    upper_rows = jnp.concatenate([top_gram, cross_gram], axis=1)
    lower_rows = jnp.concatenate([cross_gram.T, low_gram], axis=1)
    return jnp.concatenate([upper_rows, lower_rows], axis=0)


def turn_blocks(top_block, low_block, rotation):
    split = top_block.shape[1]
    new_top = jnp.dot(top_block, rotation[:split, :split], precision=highest) + jnp.dot(
        low_block, rotation[split:, :split], precision=highest
    )
    new_low = jnp.dot(top_block, rotation[:split, split:], precision=highest) + jnp.dot(
        low_block, rotation[split:, split:], precision=highest
    )
    return (new_top, new_low)


def change_partners(new_top, new_low, position, pair_count):
    outgoing = jnp.where(position == 0, new_low, new_top)
    from_left = from_behind(outgoing, "pair", 1)
    from_right = from_behind(new_low, "pair", -1)
    top_next = jnp.where(position == 0, new_top, from_left)
    low_next = jnp.where(position == pair_count - 1, new_top, from_right)
    return (top_next, low_next)


def body(snapshots):
    split = snapshots.shape[1] // 2
    pair_count = lax.axis_size("pair")
    position = lax.axis_index("pair")
    top_block = snapshots[:, :split]
    low_block = snapshots[:, split:]
    for round_index in range(ROUNDS):
        top_gram, cross_gram, low_gram = lax.psum(block_products(top_block, low_block), "row")
        gram_full = assemble(top_gram, cross_gram, low_gram)
        rotation = eigen_rotation(gram_full)
        new_top, new_low = turn_blocks(top_block, low_block, rotation)
        top_block, low_block = change_partners(new_top, new_low, position, pair_count)
    return jnp.concatenate([top_block, low_block], axis=1)


def solution(mesh):
    return jax.shard_map(
        body,
        mesh=mesh,
        in_specs=(P("row", "pair"),),
        out_specs=P("row", "pair"),
        check_vma=False,
    )
```

profile of v0, /device:TPU:6, one launch (start us, length us, event | category | flops | bytes accessed | tf_op | source)
XLA Modules:
  0.0 1160.2 jit_solution(9663790308060985377)
XLA Ops:
  6.5 4.1 fusion.4
  10.7 4.0 fusion.6
  14.7 2.4 fusion.13
  17.4 213.3 %all-reduce.12.cloned.1.call-done = (f32[128,128]{1,0:T(8,128)}, f32[128,128]{0,1:T(8,128)}, f32[128,128]{1,0:T(8,128)}) async-done(((f32[128,128]{1,0:T(8,128)}, f32[128,128]{0,1:T(8,128)}, f32[128,128]{1,0:T(8,128)}), (f32[128,128]{1,0:T(8,128)}, f32[128,128]{0,1:T(8,128)}, f32[128,128]{1,0:T(8,128)})) %all-reduce.12.cloned.1.call-update) | async-done | bytes 196624 | tf_op jit(solution)/shard_map/psum | solution.py:72
  233.7 11.7 %cholesky.298 = f32[128,128]{1,0:T(8,128)S(1)} custom-call(f32[128,128]{1,0:T(8,128)S(1)} %cholesky.498), custom_call_target="Cholesky" | custom-call | tf_op jit(solution)/shard_map/jit(cholesky)/cholesky | solution.py:25
  245.4 9.8 custom-call.21
  255.7 11.7 %cholesky.315 = f32[128,128]{1,0:T(8,128)S(1)} custom-call(f32[128,128]{1,0:T(8,128)S(1)} %convolution_subtract_fusion.11), custom_call_target="Cholesky" | custom-call | tf_op jit(solution)/shard_map/jit(cholesky)/cholesky | solution.py:25
  269.6 4.0 while.12
  273.5 20.1 %custom-call.22 = f32[2,128,128]{1,2,0:T(8,128)S(1)} custom-call(f32[2,128,128]{2,1,0:T(8,128)S(1)} %get-tuple-element.45), custom_call_target="InvertDiagBlocksLowerTriangular" | custom-call | tf_op jit(solution)/shard_map/triangular_solve/custom-call.0 | solution.py:26
  295.9 11.7 %cholesky.332 = f32[128,128]{1,0:T(8,128)S(1)} custom-call(f32[128,128]{1,0:T(8,128)S(1)} %cholesky.501), custom_call_target="Cholesky" | custom-call | tf_op jit(solution)/shard_map/jit(cholesky)/cholesky | solution.py:25
  307.7 9.8 custom-call.23
  318.0 11.7 %cholesky.349 = f32[128,128]{1,0:T(8,128)S(1)} custom-call(f32[128,128]{1,0:T(8,128)S(1)} %convolution_subtract_fusion.10), custom_call_target="Cholesky" | custom-call | tf_op jit(solution)/shard_map/jit(cholesky)/cholesky | solution.py:25
  332.5 4.3 while.13
  336.8 19.7 %custom-call.24 = f32[2,128,128]{1,2,0:T(8,128)S(1)} custom-call(f32[2,128,128]{2,1,0:T(8,128)S(1)} %get-tuple-element.46), custom_call_target="InvertDiagBlocksLowerTriangular" | custom-call | tf_op jit(solution)/shard_map/triangular_solve/custom-call.0 | solution.py:26
  360.6 2.4 broadcast_select_fusion.8
  363.0 4.9 collective-permute-start
  367.9 1.9 collective-permute-start.1
  369.9 19.1 %collective-permute-done = f32[2048,128]{0,1:T(8,128)} collective-permute-done((f32[2048,128]{0,1:T(8,128)}, f32[2048,128]{0,1:T(8,128)}, u32[]{:S(2)}, u32[]{:S(2)}) %collective-permute-start) | collective-permute-done | bytes 1048608 | tf_op jit(solution)/shard_map/ppermute | solution.py:16
  389.0 7.7 collective-permute-done.1
  403.8 206.0 %all-reduce.10.cloned.1.call-done = (f32[128,128]{1,0:T(8,128)}, f32[128,128]{0,1:T(8,128)}, f32[128,128]{1,0:T(8,128)}) async-done(((f32[128,128]{1,0:T(8,128)}, f32[128,128]{0,1:T(8,128)}, f32[128,128]{1,0:T(8,128)}), (f32[128,128]{1,0:T(8,128)}, f32[128,128]{0,1:T(8,128)}, f32[128,128]{1,0:T(8,128)})) %all-reduce.10.cloned.1.call-update) | async-done | bytes 196624 | tf_op jit(solution)/shard_map/psum | solution.py:72
  612.7 11.7 %cholesky.366 = f32[128,128]{1,0:T(8,128)S(1)} custom-call(f32[128,128]{1,0:T(8,128)S(1)} %cholesky.504), custom_call_target="Cholesky" | custom-call | tf_op jit(solution)/shard_map/jit(cholesky)/cholesky | solution.py:25
  624.5 9.8 custom-call.25
  634.8 11.7 %cholesky.383 = f32[128,128]{1,0:T(8,128)S(1)} custom-call(f32[128,128]{1,0:T(8,128)S(1)} %convolution_subtract_fusion.9), custom_call_target="Cholesky" | custom-call | tf_op jit(solution)/shard_map/jit(cholesky)/cholesky | solution.py:25
  649.2 4.0 while.14
  653.2 19.8 %custom-call.26 = f32[2,128,128]{1,2,0:T(8,128)S(1)} custom-call(f32[2,128,128]{2,1,0:T(8,128)S(1)} %get-tuple-element.47), custom_call_target="InvertDiagBlocksLowerTriangular" | custom-call | tf_op jit(solution)/shard_map/triangular_solve/custom-call.0 | solution.py:26
  675.3 11.7 %cholesky.400 = f32[128,128]{1,0:T(8,128)S(1)} custom-call(f32[128,128]{1,0:T(8,128)S(1)} %cholesky.507), custom_call_target="Cholesky" | custom-call | tf_op jit(solution)/shard_map/jit(cholesky)/cholesky | solution.py:25
  687.1 9.8 custom-call.27
  697.4 11.7 %cholesky.417 = f32[128,128]{1,0:T(8,128)S(1)} custom-call(f32[128,128]{1,0:T(8,128)S(1)} %convolution_subtract_fusion.8), custom_call_target="Cholesky" | custom-call | tf_op jit(solution)/shard_map/jit(cholesky)/cholesky | solution.py:25
  711.9 4.3 while.15
  716.2 19.7 %custom-call.28 = f32[2,128,128]{1,2,0:T(8,128)S(1)} custom-call(f32[2,128,128]{2,1,0:T(8,128)S(1)} %get-tuple-element.48), custom_call_target="InvertDiagBlocksLowerTriangular" | custom-call | tf_op jit(solution)/shard_map/triangular_solve/custom-call.0 | solution.py:26
  741.4 4.9 collective-permute-start.2
  746.3 2.4 collective-permute-start.3
  748.7 18.4 %collective-permute-done.2 = f32[2048,128]{0,1:T(8,128)S(1)} collective-permute-done((f32[2048,128]{0,1:T(8,128)S(1)}, f32[2048,128]{0,1:T(8,128)S(1)}, u32[]{:S(2)}, u32[]{:S(2)}) %collective-permute-start.2) | collective-permute-done | bytes 1048608 | tf_op jit(solution)/shard_map/ppermute | solution.py:16
  767.0 7.7 collective-permute-done.3
  779.8 206.4 %all-reduce.8.cloned.1.call-done = (f32[128,128]{1,0:T(8,128)}, f32[128,128]{0,1:T(8,128)}, f32[128,128]{1,0:T(8,128)}) async-done(((f32[128,128]{1,0:T(8,128)}, f32[128,128]{0,1:T(8,128)}, f32[128,128]{1,0:T(8,128)}), (f32[128,128]{1,0:T(8,128)}, f32[128,128]{0,1:T(8,128)}, f32[128,128]{1,0:T(8,128)})) %all-reduce.8.cloned.1.call-update) | async-done | bytes 196624 | tf_op jit(solution)/shard_map/psum | solution.py:72
  989.2 11.7 %cholesky.434 = f32[128,128]{1,0:T(8,128)S(1)} custom-call(f32[128,128]{1,0:T(8,128)S(1)} %cholesky.510), custom_call_target="Cholesky" | custom-call | tf_op jit(solution)/shard_map/jit(cholesky)/cholesky | solution.py:25
  1001.0 9.8 custom-call.29
  1011.3 11.9 %cholesky.451 = f32[128,128]{1,0:T(8,128)S(1)} custom-call(f32[128,128]{1,0:T(8,128)S(1)} %convolution_subtract_fusion.7), custom_call_target="Cholesky" | custom-call | tf_op jit(solution)/shard_map/jit(cholesky)/cholesky | solution.py:25
  1025.8 4.0 while.16
  1029.8 19.7 %custom-call.30 = f32[2,128,128]{1,2,0:T(8,128)S(1)} custom-call(f32[2,128,128]{2,1,0:T(8,128)S(1)} %get-tuple-element.49), custom_call_target="InvertDiagBlocksLowerTriangular" | custom-call | tf_op jit(solution)/shard_map/triangular_solve/custom-call.0 | solution.py:26
  1051.8 11.7 %cholesky.468 = f32[128,128]{1,0:T(8,128)S(1)} custom-call(f32[128,128]{1,0:T(8,128)S(1)} %cholesky.513), custom_call_target="Cholesky" | custom-call | tf_op jit(solution)/shard_map/jit(cholesky)/cholesky | solution.py:25
  1063.5 9.8 custom-call.31
  1073.8 11.7 %cholesky.485 = f32[128,128]{1,0:T(8,128)S(1)} custom-call(f32[128,128]{1,0:T(8,128)S(1)} %convolution_subtract_fusion.6), custom_call_target="Cholesky" | custom-call | tf_op jit(solution)/shard_map/jit(cholesky)/cholesky | solution.py:25
  1088.3 4.3 while.17
  1092.7 19.7 %custom-call.32 = f32[2,128,128]{1,2,0:T(8,128)S(1)} custom-call(f32[2,128,128]{2,1,0:T(8,128)S(1)} %get-tuple-element.50), custom_call_target="InvertDiagBlocksLowerTriangular" | custom-call | tf_op jit(solution)/shard_map/triangular_solve/custom-call.0 | solution.py:26
  1117.8 4.9 collective-permute-start.4
  1124.6 18.8 %collective-permute-done.4 = f32[2048,128]{0,1:T(8,128)S(1)} collective-permute-done((f32[2048,128]{0,1:T(8,128)S(1)}, f32[2048,128]{0,1:T(8,128)S(1)}, u32[]{:S(2)}, u32[]{:S(2)}) %collective-permute-start.4) | collective-permute-done | bytes 1048608 | tf_op jit(solution)/shard_map/ppermute | solution.py:16
  1143.5 7.7 collective-permute-done.5
  (191 shorter events, 81.6 us)
Async XLA Ops:
  6.5 8.1 copy-start
  6.5 224.2 %all-reduce.12.cloned.1.call-start = ((), (), s32[]{:S(2)}) async-start(), calls=%async_computation.2 | async-start | bytes 393216 | tf_op jit(solution)/shard_map/psum | solution.py:72
  17.1 592.7 %all-reduce.10.cloned.1.call-start = ((), (), s32[]{:S(2)}) async-start(), calls=%async_computation.1 | async-start | bytes 393216 | tf_op jit(solution)/shard_map/psum | solution.py:72
  233.6 61.1 %copy-start.1 = (f32[128,128]{0,1:T(8,128)S(1)}, f32[128,128]{0,1:T(8,128)}, u32[]{:S(2)}) copy-start(f32[128,128]{0,1:T(8,128)} %get-tuple-element.106) | copy-start | bytes 196612
  233.6 61.1 %copy-start.4 = (f32[128,128]{1,0:T(8,128)S(1)}, f32[128,128]{1,0:T(8,128)}, u32[]{:S(2)}) copy-start(f32[128,128]{1,0:T(8,128)} %get-tuple-element.105) | copy-start | bytes 196612
  233.6 61.1 %copy-start.5 = (f32[128,128]{1,0:T(8,128)S(1)}, f32[128,128]{1,0:T(8,128)}, u32[]{:S(2)}) copy-start(f32[128,128]{1,0:T(8,128)} %get-tuple-element.107) | copy-start | bytes 196612
  363.0 26.0 %collective-permute-start = (f32[2048,128]{0,1:T(8,128)}, f32[2048,128]{0,1:T(8,128)}, u32[]{:S(2)}, u32[]{:S(2)}) collective-permute-start(f32[2048,128]{0,1:T(8,128)} %get-tuple-element.154), channel_id=1, source_target_pairs={{0,32},{32,64},{64,96},{96,128},{128,160},{160,192},{192,224},{1,3... | collective-permute-start | bytes 3145736 | tf_op jit(solution)/shard_map/ppermute | solution.py:16
  367.9 28.8 %collective-permute-start.1 = (f32[2048,128]{0,1:T(8,128)}, f32[2048,128]{0,1:T(8,128)}, u32[]{:S(2)}, u32[]{:S(2)}) collective-permute-start(f32[2048,128]{0,1:T(8,128)} %get-tuple-element.155), channel_id=1, source_target_pairs={{32,0},{64,32},{96,64},{128,96},{160,128},{192,160},{224,192},{33,... | collective-permute-start | bytes 3145736 | tf_op jit(solution)/shard_map/ppermute | solution.py:16
  403.3 582.9 %all-reduce.8.cloned.1.call-start = ((), (), s32[]{:S(2)}) async-start(), calls=%async_computation | async-start | bytes 393216 | tf_op jit(solution)/shard_map/psum | solution.py:72
  612.7 61.4 %copy-start.2 = (f32[128,128]{0,1:T(8,128)S(1)}, f32[128,128]{0,1:T(8,128)}, u32[]{:S(2)}) copy-start(f32[128,128]{0,1:T(8,128)} %get-tuple-element.103) | copy-start | bytes 196612
  612.7 61.4 %copy-start.6 = (f32[128,128]{1,0:T(8,128)S(1)}, f32[128,128]{1,0:T(8,128)}, u32[]{:S(2)}) copy-start(f32[128,128]{1,0:T(8,128)} %get-tuple-element.102) | copy-start | bytes 196612
  612.7 61.4 %copy-start.7 = (f32[128,128]{1,0:T(8,128)S(1)}, f32[128,128]{1,0:T(8,128)}, u32[]{:S(2)}) copy-start(f32[128,128]{1,0:T(8,128)} %get-tuple-element.104) | copy-start | bytes 196612
  741.4 25.7 %collective-permute-start.2 = (f32[2048,128]{0,1:T(8,128)S(1)}, f32[2048,128]{0,1:T(8,128)S(1)}, u32[]{:S(2)}, u32[]{:S(2)}) collective-permute-start(f32[2048,128]{0,1:T(8,128)S(1)} %get-tuple-element.160), channel_id=1, source_target_pairs={{0,32},{32,64},{64,96},{96,128},{128,160},{160,192},{192,224},{1,3... | collective-permute-start | bytes 3145736 | tf_op jit(solution)/shard_map/ppermute | solution.py:16
  746.3 28.5 %collective-permute-start.3 = (f32[2048,128]{0,1:T(8,128)S(1)}, f32[2048,128]{0,1:T(8,128)S(1)}, u32[]{:S(2)}, u32[]{:S(2)}) collective-permute-start(f32[2048,128]{0,1:T(8,128)S(1)} %get-tuple-element.161), channel_id=1, source_target_pairs={{32,0},{64,32},{96,64},{128,96},{160,128},{192,160},{224,192},{33,... | collective-permute-start | bytes 3145736 | tf_op jit(solution)/shard_map/ppermute | solution.py:16
  989.2 61.4 %copy-start.3 = (f32[128,128]{0,1:T(8,128)S(1)}, f32[128,128]{0,1:T(8,128)}, u32[]{:S(2)}) copy-start(f32[128,128]{0,1:T(8,128)} %get-tuple-element.100) | copy-start | bytes 196612
  989.2 61.4 %copy-start.8 = (f32[128,128]{1,0:T(8,128)S(1)}, f32[128,128]{1,0:T(8,128)}, u32[]{:S(2)}) copy-start(f32[128,128]{1,0:T(8,128)} %get-tuple-element.99) | copy-start | bytes 196612
  989.2 61.4 %copy-start.9 = (f32[128,128]{1,0:T(8,128)S(1)}, f32[128,128]{1,0:T(8,128)}, u32[]{:S(2)}) copy-start(f32[128,128]{1,0:T(8,128)} %get-tuple-element.101) | copy-start | bytes 196612
  1117.8 25.7 %collective-permute-start.4 = (f32[2048,128]{0,1:T(8,128)S(1)}, f32[2048,128]{0,1:T(8,128)S(1)}, u32[]{:S(2)}, u32[]{:S(2)}) collective-permute-start(f32[2048,128]{0,1:T(8,128)S(1)} %get-tuple-element.166), channel_id=1, source_target_pairs={{0,32},{32,64},{64,96},{96,128},{128,160},{160,192},{192,224},{1,3... | collective-permute-start | bytes 3145736 | tf_op jit(solution)/shard_map/ppermute | solution.py:16
  1122.7 28.5 %collective-permute-start.5 = (f32[2048,128]{0,1:T(8,128)S(1)}, f32[2048,128]{0,1:T(8,128)S(1)}, u32[]{:S(2)}, u32[]{:S(2)}) collective-permute-start(f32[2048,128]{0,1:T(8,128)S(1)} %get-tuple-element.167), channel_id=1, source_target_pairs={{32,0},{64,32},{96,64},{128,96},{160,128},{192,160},{224,192},{33,... | collective-permute-start | bytes 3145736 | tf_op jit(solution)/shard_map/ppermute | solution.py:16
Sparse Core Ops, SparseCore 0:
  17.2 213.4 all-reduce.11
  403.4 206.3 all-reduce.9
  779.9 206.2 all-reduce.7
where the time goes:
time: 1170 us; the launch traced here: 1160 us
  waiting for transfers between devices  705 us (60%)
  other arithmetic  329 us (28%)
  matrix products  51.7 us (4%)
  local copies, waits for them, and re-layouts  29.6 us (3%)
  between operations  22.2 us (2%)
  starting transfers between devices  21.6 us (2%)
    psum x3, waiting for transfers between devices, body(): lax.psum(block_products(top_block, low_block), 'row')  626 us
    another operation x41, other arithmetic, eigen_rotation(): factor = jnp.linalg.cholesky(crossed)  207 us
    another operation x13, other arithmetic, eigen_rotation(): lax.linalg.triangular_solve(factor, images, left_side=False, lower=True,...  119 us
    ppermute x6, waiting for transfers between devices, from_behind(): return lax.ppermute(array, axis, pairs)  79.5 us
    another operation x43, local copies, waits for them, and re-layouts, eigen_rotation(): lax.linalg.triangular_solve(factor, images, left_side=False, lower=True,...  24 us
  transfers between devices with their start and end apart: 9, of which 9 were waited for; matrix products, arithmetic and copies ran while one was open for 0% of the time, Pallas kernels for 0%

commit v1 on v0

v1 whole, which is shorter than its diff:
```python
import functools

import jax
import jax.numpy as jnp
from jax import lax
from jax.experimental import pallas as pl
from jax.experimental.pallas import tpu as pltpu
from jax.sharding import PartitionSpec as P

ROUNDS = 3
BW = 128
N = 2 * BW
NB = 16
STEP = 256
MESH = pl.DeviceIdType.MESH
HIGHEST = lax.Precision.HIGHEST
VMEM = pl.BlockSpec(memory_space=pltpu.VMEM)


def product(a, b, a_dim, b_dim):
    dims = (((a_dim,), (b_dim,)), ((), ()))
    return lax.dot_general(a, b, dims, precision=HIGHEST, preferred_element_type=jnp.float32)


def eliminate(block, halves):
    extent = block.shape[0]
    rows = lax.broadcasted_iota(jnp.int32, (extent, BW), 0)
    columns = [jnp.broadcast_to(block[:, i : i + 1], (extent, BW)) for i in range(extent)]
    pivots = jnp.zeros((extent, BW), jnp.float32)
    for i in range(extent):
        pivot = columns[i][i : i + 1, :]
        pivots = jnp.where(rows == i, pivot, pivots)
        if i < extent - 1:
            factor = columns[i] * (1.0 / pivot)
            for j in range(i + 1, extent):
                columns[j] = columns[j] - factor * columns[i][j : j + 1, :]
            below = jnp.where(rows > i, factor, 0.0)
            halves = [half - below * half[i : i + 1, :] for half in halves]
        yield None
    scale = lax.rsqrt(pivots)
    yield [half * scale for half in halves]


def side_by_side(chains):
    results = [None] * len(chains)
    for step in range(NB + 1):
        for index, chain in enumerate(chains):
            results[index] = next(chain)
    return results


def solve_kernel(gram_ref, basis_ref, rest_ref):
    gram = gram_ref[...]
    rest_ref[...] = product(gram, gram, 1, 0)
    panels = N // NB
    waiting = None
    for panel in range(panels + 1):
        chains = []
        start = panel * NB
        first = BW if start >= BW else 0
        if panel < panels:
            strip = rest_ref[start : start + NB, first:]
            block = strip[:, start - first : start - first + NB]
            chains.append(eliminate(block, [strip[:, c : c + BW] for c in range(0, N - first, BW)]))
        if waiting is not None:
            done = start - NB
            strip = waiting
            if done > 0:
                earlier = basis_ref[:done, :]
                strip = strip - product(product(strip, earlier, 1, 1), earlier, 1, 0)
            block = product(strip, strip, 1, 1)
            chains.append(eliminate(block, [strip[:, :BW], strip[:, BW:]]))
        results = side_by_side(chains)
        if waiting is not None:
            basis_ref[done:start, :] = jnp.concatenate(results[-1], axis=1)
        if panel < panels:
            strip = jnp.concatenate(results[0], axis=1) if first == 0 else results[0][0]
            after = start + NB
            for low, high in ((after, after + NB), (after + NB, N)):
                if low < min(high, N):
                    rest_ref[low:high, first:] -= product(strip[:, low - first : high - first], strip, 0, 0)
            row = lax.broadcasted_iota(jnp.int32, strip.shape, 0) + start
            column = lax.broadcasted_iota(jnp.int32, strip.shape, 1) + first
            strip = jnp.where(column >= row, strip, 0.0)
            waiting = strip if first == 0 else jnp.concatenate([jnp.zeros_like(strip), strip], axis=1)


def pair_solve(gram):
    return pl.pallas_call(
        solve_kernel,
        out_shape=jax.ShapeDtypeStruct((N, N), jnp.float32),
        in_specs=[VMEM],
        out_specs=VMEM,
        scratch_shapes=[pltpu.VMEM((N, N), jnp.float32)],
        compiler_params=pltpu.CompilerParams(vmem_limit_bytes=16 * 2**20),
        name="pair_solve",
    )(gram)


def places():
    pair, row = lax.axis_index("pair"), lax.axis_index("row")
    return pair, row, lax.rem(row, 2), lax.div(row, 2)


def greet(pairs, chips, with_rows, with_pairs):
    pair, row, core, chip = places()
    barrier = pltpu.get_barrier_semaphore()
    if with_rows:
        pl.semaphore_signal(barrier, inc=1, device_id=(pair, row + 1 - 2 * core), device_id_type=MESH)

        @pl.loop(1, chips)
        def _(step):
            other = lax.rem(chip + step, chips) * 2 + core
            pl.semaphore_signal(barrier, inc=1, device_id=(pair, other), device_id_type=MESH)

    if with_pairs:

        @pl.when(pair > 0)
        def _():
            pl.semaphore_signal(barrier, inc=1, device_id=(pair - 1, row), device_id_type=MESH)

        @pl.when(pair < pairs - 1)
        def _():
            pl.semaphore_signal(barrier, inc=1, device_id=(pair + 1, row), device_id_type=MESH)

    peers = chips if with_rows else 0
    if with_pairs:
        peers = peers + jnp.where(pair > 0, 1, 0) + jnp.where(pair < pairs - 1, 1, 0)
    pl.semaphore_wait(barrier, peers)


def sum_rows(chips, part_ref, total_ref, half_ref, slots_ref, sems):
    pair, row, core, chip = places()
    piece = BW // chips
    mine = pl.multiple_of(core * BW, BW)
    theirs = pl.multiple_of(BW - core * BW, BW)
    twin = (pair, row + 1 - 2 * core)

    swap = pltpu.make_async_remote_copy(
        src_ref=part_ref.at[pl.ds(theirs, BW)], dst_ref=half_ref,
        send_sem=sems.at[0], recv_sem=sems.at[1], device_id=twin, device_id_type=MESH)
    swap.start()
    swap.wait()
    half_ref[...] += part_ref[pl.ds(mine, BW), :]

    def spread(step):
        to = lax.rem(chip + step, chips)
        return pltpu.make_async_remote_copy(
            src_ref=half_ref.at[pl.ds(pl.multiple_of(to * piece, piece), piece)], dst_ref=slots_ref.at[step - 1],
            send_sem=sems.at[2], recv_sem=sems.at[3], device_id=(pair, to * 2 + core), device_id_type=MESH)

    @pl.loop(1, chips)
    def _(step):
        spread(step).start()

    place = pl.multiple_of(chip * piece, piece)
    total = half_ref[pl.ds(place, piece), :]
    everything = slots_ref.at[pl.ds(0, chips - 1)]
    pltpu.make_async_copy(everything, everything, sems.at[3]).wait()
    total_ref[pl.ds(mine + place, piece), :] = total + jnp.sum(slots_ref[...], axis=0)
    pltpu.make_async_copy(everything, everything, sems.at[2]).wait()

    @pl.loop(1, chips)
    def _(step):
        to = lax.rem(chip + step, chips)
        here = total_ref.at[pl.ds(pl.multiple_of(mine + place, piece), piece)]
        pltpu.make_async_remote_copy(
            src_ref=here, dst_ref=here,
            send_sem=sems.at[4], recv_sem=sems.at[5], device_id=(pair, to * 2 + core), device_id_type=MESH).start()

    pltpu.make_async_copy(everything, everything, sems.at[5]).wait()
    pltpu.make_async_copy(everything, everything, sems.at[4]).wait()
    swap = pltpu.make_async_remote_copy(
        src_ref=total_ref.at[pl.ds(mine, BW)], dst_ref=total_ref.at[pl.ds(mine, BW)],
        send_sem=sems.at[6], recv_sem=sems.at[7], device_id=twin, device_id_type=MESH)
    swap.start()
    swap.wait()


def gram_kernel(chips, x_ref, total_ref, part_ref, half_ref, slots_ref, sems):
    greet(0, chips, True, False)
    part_ref[...] = jnp.zeros_like(part_ref)

    @pl.loop(0, x_ref.shape[0] // STEP)
    def _(step):
        block = x_ref[pl.ds(pl.multiple_of(step * STEP, STEP), STEP), :]
        part_ref[...] += product(block, block, 0, 0)

    sum_rows(chips, part_ref, total_ref, half_ref, slots_ref, sems)


def turn_kernel(pairs, chips, with_gram, x_ref, basis_ref, *refs):
    if with_gram:
        out_ref, total_ref, turn_ref, right_ref, left_ref, pair_sems, part_ref, half_ref, slots_ref, sems = refs
    else:
        out_ref, turn_ref, right_ref, left_ref, pair_sems = refs
    pair, row, _, _ = places()
    pieces = x_ref.shape[0] // STEP
    greet(pairs, chips, with_gram, True)
    turn_ref[...] = basis_ref[...].T

    def window(step):
        return pl.ds(pl.multiple_of(step * STEP, STEP), STEP)

    def to_right(step):
        return pltpu.make_async_remote_copy(
            src_ref=right_ref.at[window(step)], dst_ref=out_ref.at[window(step), pl.ds(0, BW)],
            send_sem=pair_sems.at[0, step], recv_sem=pair_sems.at[1, step],
            device_id=(pair + 1, row), device_id_type=MESH)

    def to_left(step):
        return pltpu.make_async_remote_copy(
            src_ref=left_ref.at[window(step)], dst_ref=out_ref.at[window(step), pl.ds(BW, BW)],
            send_sem=pair_sems.at[2, step], recv_sem=pair_sems.at[3, step],
            device_id=(pair - 1, row), device_id_type=MESH)

    @pl.loop(0, pieces)
    def _(step):
        turned = product(x_ref[window(step), :], turn_ref[...], 1, 0)
        top, low = turned[:, :BW], turned[:, BW:]
        left_ref[window(step), :] = low

        @pl.when(pair == 0)
        def _():
            right_ref[window(step), :] = low
            out_ref[window(step), pl.ds(0, BW)] = top

        @pl.when(pair > 0)
        def _():
            right_ref[window(step), :] = top
            to_left(step).start()

        @pl.when(pair == pairs - 1)
        def _():
            out_ref[window(step), pl.ds(BW, BW)] = top

        @pl.when(pair < pairs - 1)
        def _():
            to_right(step).start()

    if with_gram:
        part_ref[...] = jnp.zeros_like(part_ref)

    @pl.loop(0, pieces)
    def _(step):
        @pl.when(pair > 0)
        def _():
            to_right(step).wait_recv()

        @pl.when(pair < pairs - 1)
        def _():
            to_left(step).wait_recv()

        if with_gram:
            block = out_ref[window(step), :]
            part_ref[...] += product(block, block, 0, 0)

    if with_gram:
        sum_rows(chips, part_ref, total_ref, half_ref, slots_ref, sems)

    @pl.loop(0, pieces)
    def _(step):
        @pl.when(pair > 0)
        def _():
            to_left(step).wait_send()

        @pl.when(pair < pairs - 1)
        def _():
            to_right(step).wait_send()


def sum_scratch(chips):
    return [
        pltpu.VMEM((N, N), jnp.float32),
        pltpu.VMEM((BW, N), jnp.float32),
        pltpu.VMEM((chips - 1, BW // chips, N), jnp.float32),
        pltpu.SemaphoreType.DMA((8,)),
    ]


def params(collective_id):
    return pltpu.CompilerParams(
        collective_id=collective_id, has_side_effects=True, vmem_limit_bytes=24 * 2**20
    )


def gram_sum(x, chips):
    return pl.pallas_call(
        functools.partial(gram_kernel, chips),
        out_shape=jax.ShapeDtypeStruct((N, N), jnp.float32),
        in_specs=[VMEM],
        out_specs=VMEM,
        scratch_shapes=sum_scratch(chips),
        compiler_params=params(0),
        name="gram_sum",
    )(x)


def turn(x, basis, pairs, chips, with_gram):
    rows = x.shape[0]
    scratch = [
        pltpu.VMEM((N, N), jnp.float32),
        pltpu.VMEM((rows, BW), jnp.float32),
        pltpu.VMEM((rows, BW), jnp.float32),
        pltpu.SemaphoreType.DMA((4, rows // STEP)),
    ]
    shapes = [jax.ShapeDtypeStruct(x.shape, jnp.float32)]
    if with_gram:
        scratch += sum_scratch(chips)
        shapes.append(jax.ShapeDtypeStruct((N, N), jnp.float32))
    return pl.pallas_call(
        functools.partial(turn_kernel, pairs, chips, with_gram),
        out_shape=shapes,
        in_specs=[VMEM, VMEM],
        out_specs=[VMEM] * len(shapes),
        scratch_shapes=scratch,
        compiler_params=params(1 if with_gram else 2),
        name="turn_gram" if with_gram else "turn",
    )(x, basis)


def body(pairs, chips, x):
    gram = gram_sum(x, chips)
    for round_index in range(ROUNDS - 1):
        x, gram = turn(x, pair_solve(gram), pairs, chips, True)
    return turn(x, pair_solve(gram), pairs, chips, False)[0]


def solution(mesh):
    return jax.shard_map(
        functools.partial(body, mesh.shape["pair"], mesh.shape["row"] // 2),
        mesh=mesh,
        in_specs=(P("row", "pair"),),
        out_specs=P("row", "pair"),
        check_vma=False,
    )
```

time: 1170 us -> 202 us (0.17)
  waiting for transfers between devices: 705 us -> 0 us
  other arithmetic: 329 us -> 0 us
  Pallas kernels: 0 us -> 198 us
  matrix products: 51.7 us -> 0 us
  local copies, waits for them, and re-layouts: 29.6 us -> 2.91 us
  between operations: 22.2 us -> 0.06 us
  starting transfers between devices: 21.6 us -> 0 us
    psum x3 -> x0, waiting for transfers between devices: 626 us -> none  [body(): lax.psum(block_products(top_block, low_block), 'row')]
    another operation x54 -> x0, other arithmetic: 326 us -> none  [the longest x41 207 us: eigen_rotation(): factor = jnp.linalg.cholesky(crossed)]
    pallas_call x0 -> x7, Pallas kernels: none -> 198 us  [the longest x3 122 us: turn(): pl.pallas_call(functools.partial(turn_kernel, pairs, chips, with_gram), o...]
    ppermute x6 -> x0, waiting for transfers between devices: 79.5 us -> none  [from_behind(): return lax.ppermute(array, axis, pairs)]
    dot_general x33 -> x0, matrix products: 42.8 us -> none  [the longest x3 7.37 us: block_products(): low_gram = jnp.einsum('mi,mj->ij', low_block, low_block, precision=highest)]
    another operation x55 -> x0, local copies, waits for them, and re-layouts: 24.2 us -> none  [the longest x43 24 us: eigen_rotation(): lax.linalg.triangular_solve(factor, images, left_side=False, lower=True,...]
    ppermute x6 -> x0, starting transfers between devices: 20.9 us -> none  [from_behind(): return lax.ppermute(array, axis, pairs)]
  transfers between devices with their start and end apart: 9 -> 0, of which waited for: 9 -> 0; matrix products, arithmetic and copies ran while one was open for 0% -> 0% of each run, Pallas kernels for 0% -> 0%
where the time goes in v1:
time: 202 us; the launch traced here: 201 us
  Pallas kernels  198 us (98%)
  local copies, waits for them, and re-layouts  2.91 us (1%)
    pallas_call x3, Pallas kernels, turn(): pl.pallas_call(functools.partial(turn_kernel, pairs, chips, with_gram), o...  122 us
    pallas_call x3, Pallas kernels, pair_solve(): pl.pallas_call(solve_kernel, out_shape=jax.ShapeDtypeStruct((N, N), jnp.f...  48.9 us
    pallas_call x1, Pallas kernels, gram_sum(): pl.pallas_call(functools.partial(gram_kernel, chips), out_shape=jax.Shape...  26.6 us

profile of v1, /device:TPU:6, one launch (start us, length us, event | category | flops | bytes accessed | tf_op | source)
XLA Modules:
  0.0 200.9 jit_solution(3453149859862026214)
XLA Ops:
  0.0 0.0 copy-start
  0.0 1.6 copy-done
  1.6 26.6 %gram_sum.1.gram_ref = f32[256,256]{1,0:T(8,128)S(1)} custom-call(f32[2048,256]{1,0:T(8,128)S(1)} %copy-done), custom_call_target="tpu_custom_call" | custom-call | tf_op jit(solution)/shard_map/gram_sum/pallas_call | solution.py:288
  28.2 16.3 %pair_solve.3.basis_ref = f32[256,256]{1,0:T(8,128)S(1)} custom-call(f32[256,256]{1,0:T(8,128)S(1)} %gram_sum.1.gram_ref), custom_call_target="tpu_custom_call" | custom-call | tf_op jit(solution)/shard_map/pair_solve/pallas_call | solution.py:89
  44.5 46.4 %turn_gram.2 = (f32[2048,256]{1,0:T(8,128)S(1)}, f32[256,256]{1,0:T(8,128)S(1)}) custom-call(f32[2048,256]{1,0:T(8,128)S(1)} %copy-done, f32[256,256]{1,0:T(8,128)S(1)} %pair_solve.3.basis_ref), custom_call_target="tpu_custom_call" | custom-call | tf_op jit(solution)/shard_map/turn_gram/pallas_call | solution.py:311
  91.0 16.3 %pair_solve.4.basis_ref = f32[256,256]{1,0:T(8,128)S(1)} custom-call(f32[256,256]{1,0:T(8,128)S(1)} %get-tuple-element.10.gram_ref), custom_call_target="tpu_custom_call" | custom-call | tf_op jit(solution)/shard_map/pair_solve/pallas_call | solution.py:89
  107.3 45.9 %turn_gram.3 = (f32[2048,256]{1,0:T(8,128)S(1)}, f32[256,256]{1,0:T(8,128)S(1)}) custom-call(f32[2048,256]{1,0:T(8,128)S(1)} %get-tuple-element.9.x_ref, f32[256,256]{1,0:T(8,128)S(1)} %pair_solve.4.basis_ref), custom_call_target="tpu_custom_call" | custom-call | tf_op jit(solution)/shard_map/turn_gram/pallas_call | solution.py:311
  153.2 16.3 %pair_solve.5.basis_ref = f32[256,256]{1,0:T(8,128)S(1)} custom-call(f32[256,256]{1,0:T(8,128)S(1)} %get-tuple-element.12.gram_ref), custom_call_target="tpu_custom_call" | custom-call | tf_op jit(solution)/shard_map/pair_solve/pallas_call | solution.py:89
  169.5 30.0 %turn.1 = f32[2048,256]{1,0:T(8,128)S(1)} custom-call(f32[2048,256]{1,0:T(8,128)S(1)} %get-tuple-element.11.x_ref, f32[256,256]{1,0:T(8,128)S(1)} %pair_solve.5.basis_ref), custom_call_target="tpu_custom_call" | custom-call | tf_op jit(solution)/shard_map/turn/pallas_call | solution.py:311
  199.6 1.3 copy.3
Async XLA Ops:
  0.0 1.6 copy-start

commit v2 on v0

v2 whole, which is shorter than its diff:
```python
import functools

import jax
import jax.numpy as jnp
from jax import lax
from jax.experimental import pallas as pl
from jax.experimental.pallas import tpu as pltpu
from jax.sharding import PartitionSpec as P

ROUNDS = 3
BW = 128
N = 2 * BW
NB = 16
STEP = 256
MESH = pl.DeviceIdType.MESH
HIGHEST = lax.Precision.HIGHEST
VMEM = pl.BlockSpec(memory_space=pltpu.VMEM)


def product(a, b, a_dim, b_dim):
    dims = (((a_dim,), (b_dim,)), ((), ()))
    return lax.dot_general(a, b, dims, precision=HIGHEST, preferred_element_type=jnp.float32)


def eliminate(block, halves):
    extent = block.shape[0]
    rows = lax.broadcasted_iota(jnp.int32, (extent, BW), 0)
    columns = [jnp.broadcast_to(block[:, i : i + 1], (extent, BW)) for i in range(extent)]
    pivots = jnp.zeros((extent, BW), jnp.float32)
    for i in range(extent):
        pivot = columns[i][i : i + 1, :]
        pivots = jnp.where(rows == i, pivot, pivots)
        if i < extent - 1:
            factor = columns[i] * (1.0 / pivot)
            for j in range(i + 1, extent):
                columns[j] = columns[j] - factor * columns[i][j : j + 1, :]
            below = jnp.where(rows > i, factor, 0.0)
            halves = [half - below * half[i : i + 1, :] for half in halves]
        yield None
    scale = lax.rsqrt(pivots)
    yield [half * scale for half in halves]


def side_by_side(chains):
    results = [None] * len(chains)
    for step in range(NB + 1):
        for index, chain in enumerate(chains):
            results[index] = next(chain)
    return results


def solve(gram_ref, basis_ref, rest_ref):
    gram = gram_ref[...]
    rest_ref[...] = product(gram, gram, 1, 0)
    panels = N // NB
    waiting = None
    for panel in range(panels + 1):
        chains = []
        start = panel * NB
        first = BW if start >= BW else 0
        if panel < panels:
            strip = rest_ref[start : start + NB, first:]
            block = strip[:, start - first : start - first + NB]
            chains.append(eliminate(block, [strip[:, c : c + BW] for c in range(0, N - first, BW)]))
        if waiting is not None:
            done = start - NB
            strip = waiting
            if done > 0:
                earlier = basis_ref[:done, :]
                strip = strip - product(product(strip, earlier, 1, 1), earlier, 1, 0)
            block = product(strip, strip, 1, 1)
            chains.append(eliminate(block, [strip[:, :BW], strip[:, BW:]]))
        results = side_by_side(chains)
        if waiting is not None:
            basis_ref[done:start, :] = jnp.concatenate(results[-1], axis=1)
        if panel < panels:
            strip = jnp.concatenate(results[0], axis=1) if first == 0 else results[0][0]
            after = start + NB
            for low, high in ((after, after + NB), (after + NB, N)):
                if low < min(high, N):
                    rest_ref[low:high, first:] -= product(strip[:, low - first : high - first], strip, 0, 0)
            row = lax.broadcasted_iota(jnp.int32, strip.shape, 0) + start
            column = lax.broadcasted_iota(jnp.int32, strip.shape, 1) + first
            strip = jnp.where(column >= row, strip, 0.0)
            waiting = strip if first == 0 else jnp.concatenate([jnp.zeros_like(strip), strip], axis=1)


def places(chips):
    pair, row = lax.axis_index("pair"), lax.axis_index("row")
    depth = chips // 2
    chip = lax.div(row, 2)
    return pair, row, lax.rem(row, 2), lax.div(chip, depth), lax.rem(chip, depth)


def greet(pairs, chips):
    pair, row, core, _, _ = places(chips)
    chip = lax.div(row, 2)
    barrier = pltpu.get_barrier_semaphore()

    def call(to_pair, to_row):
        pl.semaphore_signal(barrier, inc=1, device_id=(to_pair, to_row), device_id_type=MESH)

    @pl.when(pair > 0)
    def _():
        call(pair - 1, row)

    @pl.when(pair < pairs - 1)
    def _():
        call(pair + 1, row)

    for flip in (1, 2, 3):
        call(pair, quad_row(chips, flip))

    @pl.loop(1, chips)
    def _(step):
        @pl.when(step != chips // 2)
        def _():
            call(pair, lax.rem(chip + step, chips) * 2 + core)

    neighbours = jnp.where(pair > 0, 1, 0) + jnp.where(pair < pairs - 1, 1, 0)
    return lambda: pl.semaphore_wait(barrier, neighbours + 3 + chips - 2)


def quad_row(chips, flip):
    _, _, core, y, z = places(chips)
    to_core = 1 - core if flip & 1 else core
    to_y = 1 - y if flip & 2 else y
    return (to_y * (chips // 2) + z) * 2 + to_core


def copy_to(src, dst, send_sem, recv_sem, pair, row):
    return pltpu.make_async_remote_copy(
        src_ref=src, dst_ref=dst, send_sem=send_sem, recv_sem=recv_sem,
        device_id=(pair, row), device_id_type=MESH)


def wait_bytes(ref, sem):
    pltpu.make_async_copy(ref, ref, sem).wait()


def sum_all(chips, part_ref, total_ref, half_ref, slots_ref, sems):
    pair, row, core, _, _ = places(chips)
    chip = lax.div(row, 2)
    piece = BW // chips
    mine = pl.multiple_of(core * BW, BW)
    theirs = pl.multiple_of(BW - core * BW, BW)
    twin = row + 1 - 2 * core

    swap = copy_to(part_ref.at[pl.ds(theirs, BW)], half_ref, sems.at[0], sems.at[1], pair, twin)
    swap.start()
    swap.wait()
    half_ref[...] += part_ref[pl.ds(mine, BW), :]

    @pl.loop(1, chips)
    def _(step):
        to = lax.rem(chip + step, chips)
        copy_to(half_ref.at[pl.ds(pl.multiple_of(to * piece, piece), piece)], slots_ref.at[step - 1],
                sems.at[2], sems.at[3], pair, to * 2 + core).start()

    place = pl.multiple_of(chip * piece, piece)
    total = half_ref[pl.ds(place, piece), :]
    wait_bytes(slots_ref, sems.at[3])
    here = pl.ds(pl.multiple_of(mine + place, piece), piece)
    total_ref[here, :] = total + jnp.sum(slots_ref[...], axis=0)
    wait_bytes(slots_ref, sems.at[2])

    @pl.loop(1, chips)
    def _(step):
        to = lax.rem(chip + step, chips)
        copy_to(total_ref.at[here], total_ref.at[here], sems.at[4], sems.at[5], pair, to * 2 + core).start()

    wait_bytes(slots_ref, sems.at[5])
    wait_bytes(slots_ref, sems.at[4])
    swap = copy_to(total_ref.at[pl.ds(mine, BW)], total_ref.at[pl.ds(mine, BW)], sems.at[6], sems.at[7], pair, twin)
    swap.start()
    swap.wait()


def sum_cross(chips, parity, cross_ref, total_ref, near_ref, far_ref, sems):
    pair, row, core, y, z = places(chips)
    depth = chips // 2
    quarter = BW // 4

    def of(to_core, to_y):
        return pl.ds(pl.multiple_of((to_core * 2 + to_y) * quarter, quarter), quarter)

    def others(src, dst, send, recv):
        return [copy_to(src(flip), dst(flip), send.at[flip - 1], recv.at[flip - 1], pair, quad_row(chips, flip))
                for flip in (1, 2, 3)]

    def theirs(flip):
        return cross_ref.at[of(1 - core if flip & 1 else core, 1 - y if flip & 2 else y)]

    copies = others(theirs, lambda flip: near_ref.at[flip - 1], sems.at[0], sems.at[1])
    for copy in copies:
        copy.start()
    for copy in copies:
        copy.wait_recv()
    mine = far_ref.at[parity, z]
    mine[...] = (cross_ref[of(core, y), :] + near_ref[0]) + (near_ref[1] + near_ref[2])

    @pl.loop(1, depth)
    def _(step):
        to = (y * depth + lax.rem(z + step, depth)) * 2 + core
        copy_to(mine, mine, sems.at[2, parity], sems.at[3, parity], pair, to).start()

    for copy in copies:
        copy.wait_send()
    others_far = far_ref.at[parity, pl.ds(0, depth - 1)]
    wait_bytes(others_far, sems.at[3, parity])
    total_ref[of(core, y), :] = jnp.sum(far_ref[parity], axis=0)
    here = total_ref.at[of(core, y)]
    copies = others(lambda flip: here, lambda flip: here, sems.at[4], sems.at[5])
    for copy in copies:
        copy.start()
    wait_bytes(others_far, sems.at[2, parity])
    for copy in copies:
        copy.wait_recv()
    for copy in copies:
        copy.wait_send()


def rounds_kernel(pairs, chips, x_ref, out_ref, blocks_ref, gram_ref, part_ref, half_ref, slots_ref, basis_ref,
                  rest_ref, turn_ref, right_ref, left_ref, cross_ref, total_ref, near_ref, far_ref,
                  square_ref, square_in_ref, load_sem, all_sems, cross_sems, pair_sems, square_sems):
    pair, row, _, _, _ = places(chips)
    pieces = out_ref.shape[0] // STEP
    is_first, is_last = pair == 0, pair == pairs - 1

    def window(step):
        return pl.ds(pl.multiple_of(step * STEP, STEP), STEP)

    load = pltpu.make_async_copy(x_ref, blocks_ref.at[0], load_sem)
    load.start()
    arrive = greet(pairs, chips)
    part_ref[...] = jnp.zeros_like(part_ref)
    load.wait()

    @pl.loop(0, pieces)
    def _(step):
        block = blocks_ref[0, window(step), :]
        part_ref[...] += product(block, block, 0, 0)

    arrive()
    sum_all(chips, part_ref, gram_ref, half_ref, slots_ref, all_sems)

    @pl.loop(0, ROUNDS)
    def _(turn):
        parity = lax.rem(turn, 2)
        later = 1 - parity
        old, new = blocks_ref.at[parity], blocks_ref.at[later]
        solve(gram_ref, basis_ref, rest_ref)
        turn_ref[...] = basis_ref[...].T

        def to_right(step):
            return copy_to(right_ref.at[window(step)], new.at[window(step), pl.ds(0, BW)],
                           pair_sems.at[parity, 0, step], pair_sems.at[parity, 1, step], pair + 1, row)

        def to_left(step):
            return copy_to(left_ref.at[window(step)], new.at[window(step), pl.ds(BW, BW)],
                           pair_sems.at[parity, 2, step], pair_sems.at[parity, 3, step], pair - 1, row)

        def square_right():
            return copy_to(square_ref.at[0], square_in_ref.at[parity, 0],
                           square_sems.at[parity, 0], square_sems.at[parity, 1], pair + 1, row)

        def square_left():
            return copy_to(square_ref.at[1], square_in_ref.at[parity, 1],
                           square_sems.at[parity, 2], square_sems.at[parity, 3], pair - 1, row)

        @pl.loop(0, pieces)
        def _(step):
            turned = product(old[window(step), :], turn_ref[...], 1, 0)
            top, low = turned[:, :BW], turned[:, BW:]
            left_ref[window(step), :] = low

            @pl.when(is_first)
            def _():
                right_ref[window(step), :] = low
                new[window(step), pl.ds(0, BW)] = top

            @pl.when(pair > 0)
            def _():
                right_ref[window(step), :] = top
                to_left(step).start()

            @pl.when(is_last)
            def _():
                new[window(step), pl.ds(BW, BW)] = top

            @pl.when(pair < pairs - 1)
            def _():
                to_right(step).start()

        top_rows, low_rows = basis_ref[:BW, :], basis_ref[BW:, :]
        top_square = product(product(top_rows, gram_ref[...], 1, 0), top_rows, 1, 1)
        low_square = product(product(low_rows, gram_ref[...], 1, 0), low_rows, 1, 1)
        square_ref[1] = low_square

        @pl.when(is_first)
        def _():
            square_ref[0] = low_square
            square_in_ref[parity, 0] = top_square

        @pl.when(pair > 0)
        def _():
            square_ref[0] = top_square
            square_left().start()

        @pl.when(is_last)
        def _():
            square_in_ref[parity, 1] = top_square

        @pl.when(pair < pairs - 1)
        def _():
            square_right().start()

        cross_ref[...] = jnp.zeros_like(cross_ref)

        @pl.loop(0, pieces)
        def _(step):
            @pl.when(pair > 0)
            def _():
                to_right(step).wait_recv()

            @pl.when(pair < pairs - 1)
            def _():
                to_left(step).wait_recv()

            block = new[window(step), :]
            cross_ref[...] += product(block[:, :BW], block[:, BW:], 0, 0)

        @pl.when(turn < ROUNDS - 1)
        def _():
            sum_cross(chips, parity, cross_ref, total_ref, near_ref, far_ref, cross_sems)

        @pl.when(pair > 0)
        def _():
            square_right().wait_recv()
            square_left().wait_send()

        @pl.when(pair < pairs - 1)
        def _():
            square_left().wait_recv()
            square_right().wait_send()

        total = total_ref[...]
        gram_ref[:BW, :BW] = square_in_ref[parity, 0]
        gram_ref[:BW, BW:] = total
        gram_ref[BW:, :BW] = total.T
        gram_ref[BW:, BW:] = square_in_ref[parity, 1]

        @pl.loop(0, pieces)
        def _(step):
            @pl.when(pair > 0)
            def _():
                to_left(step).wait_send()

            @pl.when(pair < pairs - 1)
            def _():
                to_right(step).wait_send()

    out_ref[...] = blocks_ref[ROUNDS % 2]


def body(pairs, chips, x):
    rows = x.shape[0]
    depth, pieces = chips // 2, rows // STEP
    f32 = jnp.float32
    square = pltpu.VMEM((N, N), f32)
    tile = pltpu.VMEM((BW, BW), f32)
    dma = pltpu.SemaphoreType.DMA
    return pl.pallas_call(
        functools.partial(rounds_kernel, pairs, chips),
        out_shape=jax.ShapeDtypeStruct(x.shape, f32),
        in_specs=[pl.BlockSpec(memory_space=pl.ANY)],
        out_specs=VMEM,
        scratch_shapes=[
            pltpu.VMEM((2, rows, N), f32),
            square,
            square,
            pltpu.VMEM((BW, N), f32),
            pltpu.VMEM((chips - 1, BW // chips, N), f32),
            square,
            square,
            square,
            pltpu.VMEM((rows, BW), f32),
            pltpu.VMEM((rows, BW), f32),
            tile,
            tile,
            pltpu.VMEM((3, BW // 4, BW), f32),
            pltpu.VMEM((2, depth, BW // 4, BW), f32),
            pltpu.VMEM((2, BW, BW), f32),
            pltpu.VMEM((2, 2, BW, BW), f32),
            dma,
            dma((8,)),
            dma((6, 3)),
            dma((2, 4, pieces)),
            dma((2, 4)),
        ],
        compiler_params=pltpu.CompilerParams(
            collective_id=0, has_side_effects=True, vmem_limit_bytes=32 * 2**20
        ),
        name="rounds",
    )(x)


def solution(mesh):
    return jax.shard_map(
        functools.partial(body, mesh.shape["pair"], mesh.shape["row"] // 2),
        mesh=mesh,
        in_specs=(P("row", "pair"),),
        out_specs=P("row", "pair"),
        check_vma=False,
    )
```

time: 1170 us -> 184 us (0.16)
  waiting for transfers between devices: 705 us -> 0 us
  other arithmetic: 329 us -> 0 us
  Pallas kernels: 0 us -> 181 us
  matrix products: 51.7 us -> 0 us
  local copies, waits for them, and re-layouts: 29.6 us -> 2.91 us
  between operations: 22.2 us -> 0.01 us
  starting transfers between devices: 21.6 us -> 0 us
    psum x3 -> x0, waiting for transfers between devices: 626 us -> none  [body(): lax.psum(block_products(top_block, low_block), 'row')]
    another operation x54 -> x0, other arithmetic: 326 us -> none  [the longest x41 207 us: eigen_rotation(): factor = jnp.linalg.cholesky(crossed)]
    pallas_call x0 -> x1, Pallas kernels: none -> 181 us  [body(): pl.pallas_call(functools.partial(rounds_kernel, pairs, chips), out_shape=...]
    ppermute x6 -> x0, waiting for transfers between devices: 79.5 us -> none  [from_behind(): return lax.ppermute(array, axis, pairs)]
    dot_general x33 -> x0, matrix products: 42.8 us -> none  [the longest x3 7.37 us: block_products(): low_gram = jnp.einsum('mi,mj->ij', low_block, low_block, precision=highest)]
    another operation x55 -> x0, local copies, waits for them, and re-layouts: 24.2 us -> none  [the longest x43 24 us: eigen_rotation(): lax.linalg.triangular_solve(factor, images, left_side=False, lower=True,...]
    ppermute x6 -> x0, starting transfers between devices: 20.9 us -> none  [from_behind(): return lax.ppermute(array, axis, pairs)]
  transfers between devices with their start and end apart: 9 -> 0, of which waited for: 9 -> 0; matrix products, arithmetic and copies ran while one was open for 0% -> 0% of each run, Pallas kernels for 0% -> 0%
where the time goes in v2:
time: 184 us
  Pallas kernels  181 us (98%)
  local copies, waits for them, and re-layouts  2.91 us (2%)
    pallas_call x1, Pallas kernels, body(): pl.pallas_call(functools.partial(rounds_kernel, pairs, chips), out_shape=...  181 us

profile of v2, /device:TPU:6, one launch (start us, length us, event | category | flops | bytes accessed | tf_op | source)
XLA Modules:
  0.0 183.8 jit_solution(3657976114355272284)
XLA Ops:
  0.0 0.0 copy-start
  0.0 1.6 copy-done
  1.6 180.8 %rounds.1 = f32[2048,256]{1,0:T(8,128)S(1)} custom-call(f32[2048,256]{1,0:T(8,128)S(1)} %copy-done), custom_call_target="tpu_custom_call" | custom-call | tf_op jit(solution)/shard_map/rounds/pallas_call | solution.py:373
  182.4 1.3 copy.3
Async XLA Ops:
  0.0 1.6 copy-start

commit v3 on v2

--- a/solution.py
+++ b/solution.py
@@ -11,7 +11,9 @@
 BW = 128
 N = 2 * BW
 NB = 16
-STEP = 256
+STEP = 128
+AHEAD = 7
+MARKS = (0, 1, 1)
 MESH = pl.DeviceIdType.MESH
 HIGHEST = lax.Precision.HIGHEST
 VMEM = pl.BlockSpec(memory_space=pltpu.VMEM)
@@ -138,7 +140,7 @@
     pltpu.make_async_copy(ref, ref, sem).wait()
 
 
-def sum_all(chips, part_ref, total_ref, half_ref, slots_ref, sems):
+def sum_all(chips, part_ref, total_ref, half_ref, slots_ref, sems, beside):
     pair, row, core, _, _ = places(chips)
     chip = lax.div(row, 2)
     piece = BW // chips
@@ -157,6 +159,8 @@
         copy_to(half_ref.at[pl.ds(pl.multiple_of(to * piece, piece), piece)], slots_ref.at[step - 1],
                 sems.at[2], sems.at[3], pair, to * 2 + core).start()
 
+    beside(0)
+
     place = pl.multiple_of(chip * piece, piece)
     total = half_ref[pl.ds(place, piece), :]
     wait_bytes(slots_ref, sems.at[3])
@@ -169,14 +173,17 @@
         to = lax.rem(chip + step, chips)
         copy_to(total_ref.at[here], total_ref.at[here], sems.at[4], sems.at[5], pair, to * 2 + core).start()
 
+    beside(1)
+
     wait_bytes(slots_ref, sems.at[5])
     wait_bytes(slots_ref, sems.at[4])
     swap = copy_to(total_ref.at[pl.ds(mine, BW)], total_ref.at[pl.ds(mine, BW)], sems.at[6], sems.at[7], pair, twin)
     swap.start()
+    beside(2)
     swap.wait()
 
 
-def sum_cross(chips, parity, cross_ref, total_ref, near_ref, far_ref, sems):
+def sum_cross(chips, parity, cross_ref, total_ref, near_ref, far_ref, sems, beside):
     pair, row, core, y, z = places(chips)
     depth = chips // 2
     quarter = BW // 4
@@ -194,6 +201,7 @@
     copies = others(theirs, lambda flip: near_ref.at[flip - 1], sems.at[0], sems.at[1])
     for copy in copies:
         copy.start()
+    beside(0)
     for copy in copies:
         copy.wait_recv()
     mine = far_ref.at[parity, z]
@@ -203,6 +211,8 @@
     def _(step):
         to = (y * depth + lax.rem(z + step, depth)) * 2 + core
         copy_to(mine, mine, sems.at[2, parity], sems.at[3, parity], pair, to).start()
+
+    beside(1)
 
     for copy in copies:
         copy.wait_send()
@@ -213,6 +223,7 @@
     copies = others(lambda flip: here, lambda flip: here, sems.at[4], sems.at[5])
     for copy in copies:
         copy.start()
+    beside(2)
     wait_bytes(others_far, sems.at[2, parity])
     for copy in copies:
         copy.wait_recv()
@@ -222,13 +233,39 @@
 
 def rounds_kernel(pairs, chips, x_ref, out_ref, blocks_ref, gram_ref, part_ref, half_ref, slots_ref, basis_ref,
                   rest_ref, turn_ref, right_ref, left_ref, cross_ref, total_ref, near_ref, far_ref,
-                  square_ref, square_in_ref, load_sem, all_sems, cross_sems, pair_sems, square_sems):
+                  square_ref, square_in_ref, ahead_ref, basis_in_ref, load_sem, all_sems, cross_sems, pair_sems,
+                  square_sems, ahead_sems, basis_sems):
     pair, row, _, _, _ = places(chips)
     pieces = out_ref.shape[0] // STEP
     is_first, is_last = pair == 0, pair == pairs - 1
 
     def window(step):
         return pl.ds(pl.multiple_of(step * STEP, STEP), STEP)
+
+    def both_ways(left, right):
+        @pl.when(pair > 0)
+        def _():
+            left()
+
+        @pl.when(pair < pairs - 1)
+        def _():
+            right()
+
+    def ahead_right(parity, step):
+        return copy_to(blocks_ref.at[parity, window(step)], ahead_ref.at[parity, 0, window(step)],
+                       ahead_sems.at[parity, 0, step], ahead_sems.at[parity, 1, step], pair + 1, row)
+
+    def ahead_left(parity, step):
+        return copy_to(blocks_ref.at[parity, window(step)], ahead_ref.at[parity, 1, window(step)],
+                       ahead_sems.at[parity, 2, step], ahead_sems.at[parity, 3, step], pair - 1, row)
+
+    def send_ahead(parity, low, high):
+        @pl.loop(low, high)
+        def _(step):
+            both_ways(lambda: ahead_left(parity, step).start(), lambda: ahead_right(parity, step).start())
+
+    def beside(parity):
+        return lambda stage: send_ahead(parity, MARKS[stage - 1] if stage else 0, MARKS[stage])
 
     load = pltpu.make_async_copy(x_ref, blocks_ref.at[0], load_sem)
     load.start()
@@ -242,22 +279,20 @@
         part_ref[...] += product(block, block, 0, 0)
 
     arrive()
-    sum_all(chips, part_ref, gram_ref, half_ref, slots_ref, all_sems)
+    sum_all(chips, part_ref, gram_ref, half_ref, slots_ref, all_sems, beside(0))
 
     @pl.loop(0, ROUNDS)
     def _(turn):
         parity = lax.rem(turn, 2)
         later = 1 - parity
         old, new = blocks_ref.at[parity], blocks_ref.at[later]
-        solve(gram_ref, basis_ref, rest_ref)
-        turn_ref[...] = basis_ref[...].T
 
         def to_right(step):
-            return copy_to(right_ref.at[window(step)], new.at[window(step), pl.ds(0, BW)],
+            return copy_to(right_ref.at[window(step - AHEAD)], new.at[window(step), pl.ds(0, BW)],
                            pair_sems.at[parity, 0, step], pair_sems.at[parity, 1, step], pair + 1, row)
 
         def to_left(step):
-            return copy_to(left_ref.at[window(step)], new.at[window(step), pl.ds(BW, BW)],
+            return copy_to(left_ref.at[window(step - AHEAD)], new.at[window(step), pl.ds(BW, BW)],
                            pair_sems.at[parity, 2, step], pair_sems.at[parity, 3, step], pair - 1, row)
 
         def square_right():
@@ -268,97 +303,114 @@
             return copy_to(square_ref.at[1], square_in_ref.at[parity, 1],
                            square_sems.at[parity, 2], square_sems.at[parity, 3], pair - 1, row)
 
-        @pl.loop(0, pieces)
+        def basis_right():
+            start = pl.multiple_of(jnp.where(is_first, BW, 0), BW)
+            return copy_to(basis_ref.at[pl.ds(start, BW)], basis_in_ref.at[parity, 0],
+                           basis_sems.at[parity, 0], basis_sems.at[parity, 1], pair + 1, row)
+
+        def basis_left():
+            return copy_to(basis_ref.at[pl.ds(BW, BW)], basis_in_ref.at[parity, 1],
+                           basis_sems.at[parity, 2], basis_sems.at[parity, 3], pair - 1, row)
+
+        send_ahead(parity, MARKS[2], AHEAD)
+        solve(gram_ref, basis_ref, rest_ref)
+
+        @pl.loop(0, AHEAD)
+        def _(step):
+            both_ways(lambda: ahead_left(parity, step).wait_send(), lambda: ahead_right(parity, step).wait_send())
+
+        both_ways(lambda: basis_left().start(), lambda: basis_right().start())
+        turn_ref[...] = basis_ref[...].T
+
+        @pl.when(is_first | is_last)
+        def _():
+            @pl.loop(0, pieces)
+            def _(step):
+                top = product(old[window(step), :], turn_ref[:, :BW], 1, 0)
+
+                @pl.when(is_first)
+                def _():
+                    new[window(step), pl.ds(0, BW)] = top
+
+                @pl.when(is_last)
+                def _():
+                    new[window(step), pl.ds(BW, BW)] = top
+
+        @pl.loop(AHEAD, pieces)
         def _(step):
             turned = product(old[window(step), :], turn_ref[...], 1, 0)
             top, low = turned[:, :BW], turned[:, BW:]
-            left_ref[window(step), :] = low
-
-            @pl.when(is_first)
-            def _():
-                right_ref[window(step), :] = low
-                new[window(step), pl.ds(0, BW)] = top
-
-            @pl.when(pair > 0)
-            def _():
-                right_ref[window(step), :] = top
-                to_left(step).start()
-
-            @pl.when(is_last)
-            def _():
-                new[window(step), pl.ds(BW, BW)] = top
-
-            @pl.when(pair < pairs - 1)
-            def _():
-                to_right(step).start()
+            left_ref[window(step - AHEAD), :] = low
+            right_ref[window(step - AHEAD), :] = jnp.where(is_first, low, top)
+            both_ways(lambda: to_left(step).start(), lambda: to_right(step).start())
 
         top_rows, low_rows = basis_ref[:BW, :], basis_ref[BW:, :]
         top_square = product(product(top_rows, gram_ref[...], 1, 0), top_rows, 1, 1)
         low_square = product(product(low_rows, gram_ref[...], 1, 0), low_rows, 1, 1)
+        square_ref[0] = jnp.where(is_first, low_square, top_square)
         square_ref[1] = low_square
+        both_ways(lambda: square_left().start(), lambda: square_right().start())
 
         @pl.when(is_first)
         def _():
-            square_ref[0] = low_square
             square_in_ref[parity, 0] = top_square
 
+        @pl.when(is_last)
+        def _():
+            square_in_ref[parity, 1] = top_square
+
+        both_ways(lambda: basis_right().wait_recv(), lambda: basis_left().wait_recv())
+        cross_ref[...] = jnp.zeros_like(cross_ref)
+
+        def add_cross(step):
+            block = new[window(step), :]
+            cross_ref[...] += product(block[:, :BW], block[:, BW:], 0, 0)
+
         @pl.when(pair > 0)
         def _():
-            square_ref[0] = top_square
-            square_left().start()
-
-        @pl.when(is_last)
-        def _():
-            square_in_ref[parity, 1] = top_square
+            turn_ref[:, :BW] = basis_in_ref[parity, 0].T
 
         @pl.when(pair < pairs - 1)
         def _():
-            square_right().start()
-
-        cross_ref[...] = jnp.zeros_like(cross_ref)
-
-        @pl.loop(0, pieces)
+            turn_ref[:, BW:] = basis_in_ref[parity, 1].T
+
+        @pl.loop(0, AHEAD)
         def _(step):
             @pl.when(pair > 0)
             def _():
-                to_right(step).wait_recv()
+                ahead_right(parity, step).wait_recv()
+                new[window(step), pl.ds(0, BW)] = product(
+                    ahead_ref[parity, 0, window(step), :], turn_ref[:, :BW], 1, 0)
 
             @pl.when(pair < pairs - 1)
             def _():
-                to_left(step).wait_recv()
-
-            block = new[window(step), :]
-            cross_ref[...] += product(block[:, :BW], block[:, BW:], 0, 0)
+                ahead_left(parity, step).wait_recv()
+                new[window(step), pl.ds(BW, BW)] = product(
+                    ahead_ref[parity, 1, window(step), :], turn_ref[:, BW:], 1, 0)
+
+            add_cross(step)
+
+        @pl.loop(AHEAD, pieces)
+        def _(step):
+            both_ways(lambda: to_right(step).wait_recv(), lambda: to_left(step).wait_recv())
+            add_cross(step)
 
         @pl.when(turn < ROUNDS - 1)
         def _():
-            sum_cross(chips, parity, cross_ref, total_ref, near_ref, far_ref, cross_sems)
-
-        @pl.when(pair > 0)
-        def _():
-            square_right().wait_recv()
-            square_left().wait_send()
-
-        @pl.when(pair < pairs - 1)
-        def _():
-            square_left().wait_recv()
-            square_right().wait_send()
-
+            sum_cross(chips, parity, cross_ref, total_ref, near_ref, far_ref, cross_sems, beside(later))
+
+        both_ways(lambda: square_right().wait_recv(), lambda: square_left().wait_recv())
+        both_ways(lambda: square_left().wait_send(), lambda: square_right().wait_send())
+        both_ways(lambda: basis_left().wait_send(), lambda: basis_right().wait_send())
         total = total_ref[...]
         gram_ref[:BW, :BW] = square_in_ref[parity, 0]
         gram_ref[:BW, BW:] = total
         gram_ref[BW:, :BW] = total.T
         gram_ref[BW:, BW:] = square_in_ref[parity, 1]
 
-        @pl.loop(0, pieces)
-        def _(step):
-            @pl.when(pair > 0)
-            def _():
-                to_left(step).wait_send()
-
-            @pl.when(pair < pairs - 1)
-            def _():
-                to_right(step).wait_send()
+        @pl.loop(AHEAD, pieces)
+        def _(step):
+            both_ways(lambda: to_left(step).wait_send(), lambda: to_right(step).wait_send())
 
     out_ref[...] = blocks_ref[ROUNDS % 2]
 
@@ -384,17 +436,21 @@
             square,
             square,
             square,
-            pltpu.VMEM((rows, BW), f32),
-            pltpu.VMEM((rows, BW), f32),
+            pltpu.VMEM((rows - AHEAD * STEP, BW), f32),
+            pltpu.VMEM((rows - AHEAD * STEP, BW), f32),
             tile,
             tile,
             pltpu.VMEM((3, BW // 4, BW), f32),
             pltpu.VMEM((2, depth, BW // 4, BW), f32),
             pltpu.VMEM((2, BW, BW), f32),
             pltpu.VMEM((2, 2, BW, BW), f32),
+            pltpu.VMEM((2, 2, AHEAD * STEP, N), f32),
+            pltpu.VMEM((2, 2, BW, N), f32),
             dma,
             dma((8,)),
             dma((6, 3)),
+            dma((2, 4, pieces)),
+            dma((2, 4)),
             dma((2, 4, pieces)),
             dma((2, 4)),
         ],

time: 184 us -> 168 us (0.913)
  Pallas kernels: 181 us -> 164 us
    pallas_call x1, Pallas kernels: 181 us -> 164 us  [body(): pl.pallas_call(functools.partial(rounds_kernel, pairs, chips), out_shape=...]
where the time goes in v3:
time: 168 us; the launch traced here: 167 us
  Pallas kernels  164 us (98%)
  local copies, waits for them, and re-layouts  2.91 us (2%)
    pallas_call x1, Pallas kernels, body(): pl.pallas_call(functools.partial(rounds_kernel, pairs, chips), out_shape=...  164 us

profile of v3, /device:TPU:6, one launch (start us, length us, event | category | flops | bytes accessed | tf_op | source)
XLA Modules:
  0.0 167.2 jit_solution(13572190212991137604)
XLA Ops:
  0.0 0.0 copy-start
  0.0 1.6 copy-done
  1.6 164.3 %rounds.1 = f32[2048,256]{1,0:T(8,128)S(1)} custom-call(f32[2048,256]{1,0:T(8,128)S(1)} %copy-done), custom_call_target="tpu_custom_call" | custom-call | tf_op jit(solution)/shard_map/rounds/pallas_call | solution.py:425
  165.9 1.3 copy.3
Async XLA Ops:
  0.0 1.6 copy-start

commit v4 on v3

--- a/solution.py
+++ b/solution.py
@@ -10,9 +10,12 @@
 ROUNDS = 3
 BW = 128
 N = 2 * BW
-NB = 16
+NB = 32
+INNER_NB = 16
+SUB = 8
+LAG = 2
 STEP = 128
-AHEAD = 7
+AHEAD = 5
 MARKS = (0, 1, 1)
 MESH = pl.DeviceIdType.MESH
 HIGHEST = lax.Precision.HIGHEST
@@ -24,23 +27,45 @@
     return lax.dot_general(a, b, dims, precision=HIGHEST, preferred_element_type=jnp.float32)
 
 
-def eliminate(block, halves):
-    extent = block.shape[0]
-    rows = lax.broadcasted_iota(jnp.int32, (extent, BW), 0)
-    columns = [jnp.broadcast_to(block[:, i : i + 1], (extent, BW)) for i in range(extent)]
-    pivots = jnp.zeros((extent, BW), jnp.float32)
-    for i in range(extent):
-        pivot = columns[i][i : i + 1, :]
-        pivots = jnp.where(rows == i, pivot, pivots)
-        if i < extent - 1:
-            factor = columns[i] * (1.0 / pivot)
-            for j in range(i + 1, extent):
-                columns[j] = columns[j] - factor * columns[i][j : j + 1, :]
-            below = jnp.where(rows > i, factor, 0.0)
-            halves = [half - below * half[i : i + 1, :] for half in halves]
-        yield None
-    scale = lax.rsqrt(pivots)
-    yield [half * scale for half in halves]
+def eliminate(block, strips):
+    groups = NB // SUB
+    rows = lax.broadcasted_iota(jnp.int32, (SUB, BW), 0)
+
+    def cut(array):
+        return [array[group * SUB : (group + 1) * SUB, :] for group in range(groups)]
+
+    block, strips = cut(block), [cut(strip) for strip in strips]
+    pivots = [jnp.zeros((SUB, BW), jnp.float32) for _ in range(groups)]
+    for start in range(0, NB, INNER_NB):
+        end = start + INNER_NB
+        columns = {
+            j: {g: jnp.broadcast_to(block[g][:, j : j + 1], (SUB, BW)) for g in range(j // SUB, groups)}
+            for j in range(start, end)
+        }
+        for i in range(start, end):
+            group, at = divmod(i, SUB)
+            pivot = columns[i][group][at : at + 1, :]
+            pivots[group] = jnp.where(rows == at, pivot, pivots[group])
+            if i < NB - 1:
+                inverse = 1.0 / pivot
+                factor = {g: columns[i][g] * inverse for g in range(group, groups)}
+                for j in range(i + 1, end):
+                    multiple = columns[i][j // SUB][j % SUB : j % SUB + 1, :]
+                    for g in range(j // SUB, groups):
+                        columns[j][g] = columns[j][g] - factor[g] * multiple
+                factor[group] = jnp.where(rows > at, factor[group], 0.0)
+                below = range((i + 1) // SUB, groups)
+                for strip in strips:
+                    line = strip[group][at : at + 1, :]
+                    for g in below:
+                        strip[g] = strip[g] - factor[g] * line
+                if end < NB:
+                    line = block[group][at : at + 1, :]
+                    for g in below:
+                        block[g] = block[g] - factor[g][:, :NB] * line
+            yield None
+    scale = [lax.rsqrt(pivot) for pivot in pivots]
+    yield [jnp.concatenate([x * y for x, y in zip(strip, scale)], axis=0) for strip in strips]
 
 
 def side_by_side(chains):
@@ -51,30 +76,36 @@
     return results
 
 
-def solve(gram_ref, basis_ref, rest_ref):
+def solve(gram_ref, basis_ref, rest_ref, factor_ref):
     gram = gram_ref[...]
     rest_ref[...] = product(gram, gram, 1, 0)
     panels = N // NB
-    waiting = None
-    for panel in range(panels + 1):
+    freed = last = None
+    for panel in range(panels + LAG):
         chains = []
-        start = panel * NB
+        start, behind = panel * NB, panel - LAG
         first = BW if start >= BW else 0
         if panel < panels:
             strip = rest_ref[start : start + NB, first:]
             block = strip[:, start - first : start - first + NB]
             chains.append(eliminate(block, [strip[:, c : c + BW] for c in range(0, N - first, BW)]))
-        if waiting is not None:
-            done = start - NB
-            strip = waiting
-            if done > 0:
-                earlier = basis_ref[:done, :]
-                strip = strip - product(product(strip, earlier, 1, 1), earlier, 1, 0)
+        if behind >= 0:
+            strip = freed
             block = product(strip, strip, 1, 1)
+            if behind > 0:
+                share = product(strip, last, 1, 1)
+                block = block - product(share, share, 1, 1)
+                strip = strip - product(share, last, 1, 0)
             chains.append(eliminate(block, [strip[:, :BW], strip[:, BW:]]))
+        if 0 <= behind + 1 < panels:
+            freed = factor_ref[(behind + 1) * NB : (behind + 2) * NB, :]
+            if behind > 0:
+                earlier = basis_ref[: behind * NB, :]
+                freed = freed - product(product(freed, earlier, 1, 1), earlier, 1, 0)
         results = side_by_side(chains)
-        if waiting is not None:
-            basis_ref[done:start, :] = jnp.concatenate(results[-1], axis=1)
+        if behind >= 0:
+            last = jnp.concatenate(results[-1], axis=1)
+            basis_ref[behind * NB : (behind + 1) * NB, :] = last
         if panel < panels:
             strip = jnp.concatenate(results[0], axis=1) if first == 0 else results[0][0]
             after = start + NB
@@ -84,7 +115,8 @@
             row = lax.broadcasted_iota(jnp.int32, strip.shape, 0) + start
             column = lax.broadcasted_iota(jnp.int32, strip.shape, 1) + first
             strip = jnp.where(column >= row, strip, 0.0)
-            waiting = strip if first == 0 else jnp.concatenate([jnp.zeros_like(strip), strip], axis=1)
+            strip = strip if first == 0 else jnp.concatenate([jnp.zeros_like(strip), strip], axis=1)
+            factor_ref[start : start + NB, :] = strip
 
 
 def places(chips):
@@ -232,7 +264,7 @@
 
 
 def rounds_kernel(pairs, chips, x_ref, out_ref, blocks_ref, gram_ref, part_ref, half_ref, slots_ref, basis_ref,
-                  rest_ref, turn_ref, right_ref, left_ref, cross_ref, total_ref, near_ref, far_ref,
+                  rest_ref, factor_ref, turn_ref, right_ref, left_ref, cross_ref, total_ref, near_ref, far_ref,
                   square_ref, square_in_ref, ahead_ref, basis_in_ref, load_sem, all_sems, cross_sems, pair_sems,
                   square_sems, ahead_sems, basis_sems):
     pair, row, _, _, _ = places(chips)
@@ -313,7 +345,7 @@
                            basis_sems.at[parity, 2], basis_sems.at[parity, 3], pair - 1, row)
 
         send_ahead(parity, MARKS[2], AHEAD)
-        solve(gram_ref, basis_ref, rest_ref)
+        solve(gram_ref, basis_ref, rest_ref, factor_ref)
 
         @pl.loop(0, AHEAD)
         def _(step):
@@ -433,6 +465,7 @@
             square,
             pltpu.VMEM((BW, N), f32),
             pltpu.VMEM((chips - 1, BW // chips, N), f32),
+            square,
             square,
             square,
             square,

time: 168 us -> 160 us (0.952)
  Pallas kernels: 164 us -> 156 us
    pallas_call x1, Pallas kernels: 164 us -> 156 us  [body(): pl.pallas_call(functools.partial(rounds_kernel, pairs, chips), out_shape=...]
where the time goes in v4:
time: 160 us; the launch traced here: 159 us
  Pallas kernels  156 us (98%)
  local copies, waits for them, and re-layouts  2.91 us (2%)
    pallas_call x1, Pallas kernels, body(): pl.pallas_call(functools.partial(rounds_kernel, pairs, chips), out_shape=...  156 us

profile of v4, /device:TPU:6, one launch (start us, length us, event | category | flops | bytes accessed | tf_op | source)
XLA Modules:
  0.0 158.9 jit_solution(7731847016560042774)
XLA Ops:
  0.0 0.0 copy-start
  0.0 1.6 copy-done
  1.6 156.0 %rounds.1 = f32[2048,256]{1,0:T(8,128)S(1)} custom-call(f32[2048,256]{1,0:T(8,128)S(1)} %copy-done), custom_call_target="tpu_custom_call" | custom-call | tf_op jit(solution)/shard_map/rounds/pallas_call | solution.py:457
  157.6 1.3 copy.3
Async XLA Ops:
  0.0 1.6 %copy-start = (f32[2048,256]{1,0:T(8,128)S(1)}, f32[2048,256]{1,0:T(8,128)}, u32[]{:S(2)}) copy-start(f32[2048,256]{1,0:T(8,128)} %x_ref.1) | copy-start | bytes 6291460

commit v5 on v4

--- a/solution.py
+++ b/solution.py
@@ -14,9 +14,9 @@
 INNER_NB = 16
 SUB = 8
 LAG = 2
-STEP = 128
-AHEAD = 5
-MARKS = (0, 1, 1)
+STEP = 256
+AHEAD = 2
+MARKS = (0, 0, 1)
 MESH = pl.DeviceIdType.MESH
 HIGHEST = lax.Precision.HIGHEST
 VMEM = pl.BlockSpec(memory_space=pltpu.VMEM)

time: 160 us -> 158 us (0.988)
  no operation moved by 1% of the time
where the time goes in v5:
time: 158 us
  Pallas kernels  155 us (98%)
  local copies, waits for them, and re-layouts  2.91 us (2%)
    pallas_call x1, Pallas kernels, body(): pl.pallas_call(functools.partial(rounds_kernel, pairs, chips), out_shape=...  155 us

profile of v5, /device:TPU:6, one launch (start us, length us, event | category | flops | bytes accessed | tf_op | source)
XLA Modules:
  0.0 158.3 jit_solution(366033088034935306)
XLA Ops:
  0.0 0.0 copy-start
  0.0 1.6 %copy-done = f32[2048,256]{1,0:T(8,128)S(1)} copy-done((f32[2048,256]{1,0:T(8,128)S(1)}, f32[2048,256]{1,0:T(8,128)}, u32[]{:S(2)}) %copy-start) | copy-done | bytes 2097176
  1.6 155.4 %rounds.1 = f32[2048,256]{1,0:T(8,128)S(1)} custom-call(f32[2048,256]{1,0:T(8,128)S(1)} %copy-done), custom_call_target="tpu_custom_call" | custom-call | tf_op jit(solution)/shard_map/rounds/pallas_call | solution.py:457
  157.0 1.3 copy.3
Async XLA Ops:
  0.0 1.6 %copy-start = (f32[2048,256]{1,0:T(8,128)S(1)}, f32[2048,256]{1,0:T(8,128)}, u32[]{:S(2)}) copy-start(f32[2048,256]{1,0:T(8,128)} %x_ref.1) | copy-start | bytes 6291460
